TPU v7x, 32 devices: a whole 2x2x4 slice. The times are simulated.
32 devices in a mesh: rep: 8 (over y, x, core), exp: 4 (over z).
Axes of the slice: x: 2, y: 2, z: 4, core: 2. Of those that a mesh axis runs over, the one named last changes fastest.
Arguments:
- tokens: bfloat16 [4096, 2048], P(('rep', 'exp')), may hold values from -6 to 6
- expert_ids: int32 [4096, 8], P(('rep', 'exp')), may hold values from 0 to 15, all different within a row; in each aligned block of 128 rows (0 to 127, 128 to 255, ...) at most 72 rows name the same one
- route_weights: float32 [4096, 8], P(('rep', 'exp')), may hold values from 0.05 to 1
- placement_map: int32 [16], replicated, may hold values from 0 to 15, each once
- w_gate: bfloat16 [16, 2048, 384], P('exp', 'rep'), may hold values from -0.125 to 0.125
- w_up: bfloat16 [16, 2048, 384], P('exp', 'rep'), may hold values from -0.125 to 0.125
- down_rows: bfloat16 [16, 2048, 384], P('exp', 'rep'), may hold values from -0.3125 to 0.3125
Outputs:
- mixed: bfloat16 [4096, 2048], P(('rep', 'exp'))
Inputs may be any that keep to these rules, and one draw needn't show every extreme that they name: `expert_ids`: each row names 8 different experts. Within each device's aligned block of 128 rows no expert is named by more than 72 rows, a bound that some block reaches. `placement_map`: A permutation: every storage index is used once.
All inputs are finite; a program needn't handle non-finite values.
Results may differ from a plain program's by a relative error of at most 0.0057.
Values may be sent and summed in bfloat16 or wider, within the bound.
A program may use at most 64 MiB of HBM per device.

v0:
```python
import jax
import jax.numpy as jnp
from jax import lax
from jax.sharding import PartitionSpec as P

CAP = 72


def apply_experts(received, weights):
    sources, local_count, capacity, model_width = received.shape
    results = []
    for member in range(local_count):
        row_block = received[:, member].reshape(-1, model_width)
        gate_value = jnp.dot(row_block, weights[0, member], preferred_element_type=jnp.float32)
        up_value = jnp.dot(row_block, weights[1, member], preferred_element_type=jnp.float32)
        hidden = (jax.nn.silu(gate_value) * up_value).astype(jnp.bfloat16)
        result = lax.dot_general(
            hidden, weights[2, member], (((1,), (1,)), ((), ())), preferred_element_type=jnp.float32
        )
        results.append(result.astype(jnp.bfloat16).reshape(sources, capacity, model_width))
    return jnp.stack(results, axis=1)


def on_device(tokens, expert_ids, route_weights, placement_map, w_gate, w_up, down_rows):
    tok_rows, top_count = expert_ids.shape
    experts = placement_map.shape[0]
    local_experts = w_gate.shape[0]
    model_width = tokens.shape[1]
    groups = lax.axis_size("exp")
    expert_range = jnp.arange(experts, dtype=jnp.int32)
    slot_ids = jnp.sum(jnp.where(expert_ids[:, :, None] == expert_range, placement_map, 0), axis=2)
    flat_slots = slot_ids.reshape(-1)
    onehot = (flat_slots[:, None] == expert_range).astype(jnp.int32)
    position = jnp.sum((jnp.cumsum(onehot, axis=0) - 1) * onehot, axis=1)
    target = flat_slots * CAP + position
    row_owner = jnp.arange(tok_rows * top_count, dtype=jnp.int32) // top_count
    source = jnp.full((experts * CAP,), tok_rows, jnp.int32).at[target].set(row_owner)
    outgoing = jnp.take(tokens, source, axis=0, mode="fill", fill_value=0)
    outgoing = outgoing.reshape(groups, local_experts, CAP, model_width)
    stacked = jnp.stack([w_gate, w_up, down_rows])
    stacked = lax.all_gather(stacked, "rep", axis=2, tiled=True)
    received = lax.all_to_all(outgoing, "exp", split_axis=0, concat_axis=0, tiled=True)
    returned = lax.all_to_all(
        apply_experts(received, stacked), "exp", split_axis=0, concat_axis=0, tiled=True
    )
    returned = returned.reshape(experts * CAP, model_width)
    picked = jnp.take(returned, target, axis=0).reshape(tok_rows, top_count, model_width)
    mixed = jnp.sum(route_weights[:, :, None] * picked.astype(jnp.float32), axis=1)
    return mixed.astype(jnp.bfloat16)


def solution(mesh):
    return jax.shard_map(
        on_device,
        mesh=mesh,
        in_specs=(
            P(("rep", "exp"), None),
            P(("rep", "exp"), None),
            P(("rep", "exp"), None),
            P(),
            P("exp", "rep", None),
            P("exp", "rep", None),
            P("exp", "rep", None),
        ),
        out_specs=P(("rep", "exp"), None),
        check_vma=False,
    )
```

profile of v0, /device:TPU:0, one launch (start us, length us, event | category | flops | bytes accessed | tf_op | source)
XLA Modules:
  0.0 307.0 jit_solution(1008810608501550227)
XLA Ops:
  6.5 3.5 %pad_maximum_fusion.1 = bf16[3,4,256,384]{3,2,1,0:T(8,128)(2,1)} fusion(bf16[1,4,256,384]{3,2,1,0:T(8,128)(2,1)} %bitcast.122, bf16[1,4,256,384]{3,2,1,0:T(8,128)(2,1)} %bitcast.123, bf16[1,4,256,384]{3,2,1,0:T(8,128)(2,1)} %bitcast.124), kind=kLoop, calls=%fused_computation.11 | loop fusion | flops 2359296 | bytes 4718592 | tf_op jit(solution)/shard_map/stack | solution.py:40
  10.0 0.7 copy-done.3
  10.8 0.1 copy.27
  10.9 0.1 eq.42
  11.0 0.1 reshape.81
  11.1 4.5 %reduce-window.6 = s32[16,8,128]{2,1,0:T(8,128)S(1)} reduce-window(s32[16,8,128]{2,1,0:T(8,128)S(1)} %fusion.42, s32[]{:T(128)} %constant.54.clone.1), window={size=1x1x128 pad=0_0x0_0x127_0}, to_apply=%region_1.2 | reduce-window | flops 2080768 | bytes 131076 | tf_op jit(solution)/shard_map/reduce-window
  15.6 0.1 slice.76
  15.7 0.1 copy.29
  15.9 0.1 copy.33
  16.0 0.1 mul.59
  16.1 0.1 add_add_fusion
  16.3 4.3 %scatter_custom_fusion = s32[1152]{0:T(1024)S(1)} fusion(s32[1024]{0:T(1024)S(1)} %bitcast.128, s32[1024]{0:T(1024)S(1)} %add_select_fusion, s32[]{:T(128)} %constant.59.clone.1), kind=kCustom, calls=%fused_computation.84 | custom fusion | bytes 4612 | tf_op jit(solution)/shard_map/scatter | solution.py:37
  20.6 0.1 broadcast_in_dim.44
  20.7 5.9 %gather_fusion = bf16[1152,2048]{1,0:T(8,128)(2,1)} fusion(bf16[128,2048]{1,0:T(8,128)(2,1)S(1)} %copy-done, s32[2048]{0:T(1024)S(1)} %pad_clamp_fusion), kind=kCustom, calls=%fused_computation | custom fusion | bytes 9441792 | tf_op jit(solution)/shard_map/jit(_take)/gather | solution.py:38
  26.7 2.7 broadcast_select_fusion
  29.4 110.5 %all_to_all.10 = bf16[4,4,72,2048]{3,2,1,0:T(8,128)(2,1)S(1)} all-to-all(bf16[4,4,72,2048]{3,2,1,0:T(8,128)(2,1)S(1)} %broadcast_select_fusion), channel_id=1, replica_groups=mesh['rep'=8,'exp'=4] {'exp'}, dimensions={0} | all-to-all | bytes 9437184 | tf_op jit(solution)/shard_map/all_to_all | solution.py:42
  139.9 1.9 fusion.52
  141.8 2.5 fusion.7
  144.3 4.7 %convolution_convert_fusion.3 = bf16[288,2048]{1,0:T(8,128)(2,1)} fusion(bf16[3,4,2048,384]{3,2,1,0:T(8,128)(2,1)} %all-gather.2.cloned.1.call-done, bf16[288,2048]{1,0:T(8,128)(2,1)} %bitcast.119, f32[288,384]{1,0:T(8,128)S(1)} %fusion.7), kind=kOutput, calls=%fused_computation.10 | convolution fusion | flops 907223040 | bytes 5947392 | tf_op jit(solution)/shard_map/dot_general | solution.py:17
  149.1 2.5 fusion.5
  151.6 4.7 %convolution_convert_fusion.2 = bf16[288,2048]{1,0:T(8,128)(2,1)} fusion(bf16[3,4,2048,384]{3,2,1,0:T(8,128)(2,1)} %all-gather.2.cloned.1.call-done, bf16[288,2048]{1,0:T(8,128)(2,1)} %bitcast.116, f32[288,384]{1,0:T(8,128)S(1)} %fusion.5), kind=kOutput, calls=%fused_computation.9 | convolution fusion | flops 907223040 | bytes 5947392 | tf_op jit(solution)/shard_map/dot_general | solution.py:17
  156.4 2.2 fusion.3
  158.6 4.4 %convolution_convert_fusion.1 = bf16[288,2048]{1,0:T(8,128)(2,1)} fusion(bf16[3,4,2048,384]{3,2,1,0:T(8,128)(2,1)} %all-gather.2.cloned.1.call-done, bf16[288,2048]{1,0:T(8,128)(2,1)S(1)} %bitcast.113, f32[288,384]{1,0:T(8,128)S(1)} %fusion.3), kind=kOutput, calls=%fused_computation.8 | convolution fusion | flops 907223040 | bytes 5947392 | tf_op jit(solution)/shard_map/dot_general | solution.py:17
  162.9 2.2 fusion.1
  165.1 4.5 %convolution_convert_fusion = bf16[288,2048]{1,0:T(8,128)(2,1)} fusion(bf16[3,4,2048,384]{3,2,1,0:T(8,128)(2,1)} %all-gather.2.cloned.1.call-done, bf16[288,2048]{1,0:T(8,128)(2,1)S(1)} %bitcast.111, f32[288,384]{1,0:T(8,128)S(1)} %fusion.1), kind=kOutput, calls=%fused_computation.7 | convolution fusion | flops 907223040 | bytes 5947392 | tf_op jit(solution)/shard_map/dot_general | solution.py:17
  169.6 3.8 %pad_maximum_fusion = bf16[4,4,72,2048]{3,2,1,0:T(8,128)(2,1)} fusion(bf16[4,1,72,2048]{3,2,1,0:T(8,128)(2,1)} %bitcast.121, bf16[4,1,72,2048]{3,2,1,0:T(8,128)(2,1)} %bitcast.120, bf16[4,1,72,2048]{3,2,1,0:T(8,128)(2,1)} %bitcast.117, bf16[4,1,72,2048]{3,2,1,0:T(8,128)(2,1)S(1)} %bitcast.114), kind=kLoop, calls=%fused_computation.4 | loop fusion | flops 7077888 | bytes 9437184 | tf_op jit(solution)/shard_map/stack | solution.py:21
  173.4 5.3 %all-to-all-start.1 = ((bf16[4,4,72,2048]{3,2,1,0:T(8,128)(2,1)}), bf16[4,4,72,2048]{3,2,1,0:T(8,128)(2,1)}, u32[]{:S(2)}, u32[]{:S(2)}) async-start(bf16[4,4,72,2048]{3,2,1,0:T(8,128)(2,1)} %pad_maximum_fusion), calls=%async_computation.1 | async-start | bytes 9437184 | tf_op jit(solution)/shard_map/all_to_all | solution.py:43
  178.9 0.1 copy.32
  179.0 0.1 copy.26
  179.1 103.0 %all-to-all-done.1 = bf16[4,4,72,2048]{3,2,1,0:T(8,128)(2,1)} async-done(((bf16[4,4,72,2048]{3,2,1,0:T(8,128)(2,1)}), bf16[4,4,72,2048]{3,2,1,0:T(8,128)(2,1)}, u32[]{:S(2)}, u32[]{:S(2)}) %all-to-all-start.1) | async-done | bytes 4718624 | tf_op jit(solution)/shard_map/all_to_all | solution.py:43
  282.1 11.8 %gather_fusion.1 = bf16[1024,2048]{1,0:T(8,128)(2,1)} fusion(bf16[1152,2048]{1,0:T(8,128)(2,1)} %bitcast.32, s32[1024]{0:T(1024)S(1)} %broadcast_clamp_fusion), kind=kCustom, calls=%fused_computation.1 | custom fusion | bytes 8392704 | tf_op jit(solution)/shard_map/jit(_take)/gather | solution.py:47
  293.9 6.3 %multiply_reduce_fusion = bf16[128,2048]{1,0:T(8,128)(2,1)} fusion(bf16[1024,2048]{1,0:T(8,128)(2,1)} %gather_fusion.1, f32[128,8]{1,0:T(8,128)S(1)} %copy.26, pred[128,8]{1,0:T(8,128)(4,1)S(1)} %copy.32), kind=kLoop, calls=%fused_computation.3 | loop fusion | flops 8126464 | bytes 4723712 | tf_op jit(solution)/shard_map/reduce_sum | solution.py:48
  (28 shorter events, 0.4 us)
Async XLA Ops:
  6.5 14.2 %copy-start = (bf16[128,2048]{1,0:T(8,128)(2,1)S(1)}, bf16[128,2048]{1,0:T(8,128)(2,1)}, u32[]{:S(2)}) copy-start(bf16[128,2048]{1,0:T(8,128)(2,1)} %param.7) | copy-start | bytes 1572868
  6.5 135.3 %all-gather.2.cloned.1.call-start = ((), (), s32[]{:S(2)}) async-start(), calls=%async_computation.2 | async-start | bytes 21233664 | tf_op jit(solution)/shard_map/all_gather | solution.py:41
  10.0 0.7 copy-start.3
  10.0 0.7 copy-start.4
  165.1 4.5 %copy-start.1 = (bf16[288,2048]{1,0:T(8,128)(2,1)S(1)}, bf16[288,2048]{1,0:T(8,128)(2,1)}, u32[]{:S(2)}) copy-start(bf16[288,2048]{1,0:T(8,128)(2,1)} %convolution_convert_fusion.3) | copy-start | bytes 3538948
  173.4 5.6 %copy-start.2 = (f32[128,8]{0,1:T(8,128)S(1)}, f32[128,8]{0,1:T(8,128)}, u32[]{:S(2)}) copy-start(f32[128,8]{0,1:T(8,128)} %param.9) | copy-start | bytes 12292
  173.4 108.7 %all-to-all-start.1 = ((bf16[4,4,72,2048]{3,2,1,0:T(8,128)(2,1)}), bf16[4,4,72,2048]{3,2,1,0:T(8,128)(2,1)}, u32[]{:S(2)}, u32[]{:S(2)}) async-start(bf16[4,4,72,2048]{3,2,1,0:T(8,128)(2,1)} %pad_maximum_fusion), calls=%async_computation.1 | async-start | bytes 9437184 | tf_op jit(solution)/shard_map/all_to_all | solution.py:43
Sparse Core Ops, SparseCore 0:
  10.1 101.4 all-gather.1
where the time goes:
time: 308 us; the launch traced here: 307 us
  blocking collectives  110 us (36%)
  waiting for transfers between devices  103 us (33%)
  matrix products  27.7 us (9%)
  local copies, waits for them, and re-layouts  25.8 us (8%)
  other arithmetic  21.1 us (7%)
  between operations  13.6 us (4%)
  starting transfers between devices  5.29 us (2%)
    all_to_all x1, blocking collectives, on_device(): lax.all_to_all(outgoing, 'exp', split_axis=0, concat_axis=0, tiled=True)  110 us
    all_to_all x1, waiting for transfers between devices, on_device(): lax.all_to_all(apply_experts(received, stacked), 'exp', split_axis=0, con...  103 us
    dot_general x4, matrix products, apply_experts(): lax.dot_general(hidden, weights[2, member], (((1,), (1,)), ((), ())), pre...  18.3 us
    gather x1, local copies, waits for them, and re-layouts, on_device(): jnp.take(returned, target, axis=0).reshape(tok_rows, top_count, model_width)  11.8 us
    dot_general x4, matrix products, apply_experts(): jnp.dot(row_block, weights[0, member], preferred_element_type=jnp.float32)  9.41 us
    reduce_sum x1, other arithmetic, on_device(): jnp.sum(route_weights[:, :, None] * picked.astype(jnp.float32), axis=1)  6.27 us
  transfers between devices with their start and end apart: 2, of which 1 were waited for; matrix products, arithmetic and copies ran while one was open for 7% of the time, Pallas kernels for 0%

commit v1 on v0

v1 whole, which is shorter than its diff:
```python
import jax
import jax.numpy as jnp
from jax import lax
from jax.sharding import PartitionSpec as P


def on_device(tokens, expert_ids, route_weights, placement_map, w_gate, w_up, down_rows):
    experts = placement_map.shape[0]
    local_experts, _, width = w_gate.shape
    model_width = tokens.shape[1]
    expert_range = jnp.arange(experts, dtype=jnp.int32)
    slot_ids = jnp.sum(jnp.where(expert_ids[:, :, None] == expert_range, placement_map, 0), axis=2)
    share = jnp.sum(
        jnp.where(slot_ids[:, :, None] == expert_range, route_weights[:, :, None], 0.0), axis=1
    )
    rows = lax.all_gather(tokens, "exp", axis=0, tiled=True)
    share = lax.all_gather(share, "exp", axis=0, tiled=True)
    share = lax.dynamic_slice_in_dim(share, lax.axis_index("exp") * local_experts, local_experts, 1)
    gate_up = lax.all_gather(jnp.stack([w_gate, w_up]), "rep", axis=2, tiled=True)
    down = lax.all_gather(down_rows, "rep", axis=1, tiled=True)
    parts = []
    for member in range(local_experts):
        gate_value = jnp.dot(rows, gate_up[0, member], preferred_element_type=jnp.float32)
        up_value = jnp.dot(rows, gate_up[1, member], preferred_element_type=jnp.float32)
        hidden = jax.nn.silu(gate_value) * up_value * share[:, member : member + 1]
        parts.append(hidden.astype(jnp.bfloat16))
    total = 0.0
    for member in range(local_experts):
        total = total + lax.dot_general(
            parts[member], down[member], (((1,), (1,)), ((), ())), preferred_element_type=jnp.float32
        )
    mixed = lax.psum_scatter(total.astype(jnp.bfloat16), "exp", scatter_dimension=0, tiled=True)
    return mixed.astype(jnp.bfloat16)


def solution(mesh):
    return jax.shard_map(
        on_device,
        mesh=mesh,
        in_specs=(
            P(("rep", "exp"), None),
            P(("rep", "exp"), None),
            P(("rep", "exp"), None),
            P(),
            P("exp", "rep", None),
            P("exp", "rep", None),
            P("exp", "rep", None),
        ),
        out_specs=P(("rep", "exp"), None),
        check_vma=False,
    )
```

time: 308 us -> 257 us (0.83)
  blocking collectives: 110 us -> 14.9 us
  waiting for transfers between devices: 103 us -> 184 us
  local copies, waits for them, and re-layouts: 25.8 us -> 0.03 us
  other arithmetic: 21.1 us -> 2.83 us
  matrix products: 27.7 us -> 41.7 us
  starting transfers between devices: 5.29 us -> 0.12 us
    all_gather x1 -> x3, waiting for transfers between devices: 0.01 us -> 139 us  [the longest x1 72.8 us: on_device(): lax.all_gather(jnp.stack([w_gate, w_up]), 'rep', axis=2, tiled=True)]
    all_to_all x1 -> x0, blocking collectives: 110 us -> none  [on_device(): lax.all_to_all(outgoing, 'exp', split_axis=0, concat_axis=0, tiled=True)]
    all_to_all x1 -> x0, waiting for transfers between devices: 103 us -> none  [on_device(): lax.all_to_all(apply_experts(received, stacked), 'exp', split_axis=0, con...]
    reduce_scatter x0 -> x1, waiting for transfers between devices: none -> 44 us  [on_device(): lax.psum_scatter(total.astype(jnp.bfloat16), 'exp', scatter_dimension=0,...]
    gather x2 -> x0, local copies, waits for them, and re-layouts: 17.7 us -> none  [the longest x1 11.8 us: on_device(): jnp.take(returned, target, axis=0).reshape(tok_rows, top_count, model_width)]
    all_gather x0 -> x1, blocking collectives: none -> 14.9 us  [on_device(): share = lax.all_gather(share, 'exp', axis=0, tiled=True)]
    dot_general x8, matrix products: 27.7 us -> 41.7 us  [the longest x4 28.5 us: on_device(): lax.dot_general(parts[member], down[member], (((1,), (1,)), ((), ())), pr...]
    another operation x4 -> x1, other arithmetic: 11.8 us -> 2.73 us  [on_device(): jnp.stack([w_gate, w_up])]
  transfers between devices with their start and end apart: 2 -> 4, of which waited for: 1 -> 4; matrix products, arithmetic and copies ran while one was open for 7% -> 6% of each run, Pallas kernels for 0% -> 0%
where the time goes in v1:
time: 257 us
  waiting for transfers between devices  184 us (72%)
  matrix products  41.7 us (16%)
  blocking collectives  14.9 us (6%)
  between operations  13.2 us (5%)
  other arithmetic  2.83 us (1%)
    all_gather x1, waiting for transfers between devices, on_device(): lax.all_gather(jnp.stack([w_gate, w_up]), 'rep', axis=2, tiled=True)  72.8 us
    reduce_scatter x1, waiting for transfers between devices, on_device(): lax.psum_scatter(total.astype(jnp.bfloat16), 'exp', scatter_dimension=0,...  44 us
    all_gather x1, waiting for transfers between devices, on_device(): down = lax.all_gather(down_rows, 'rep', axis=1, tiled=True)  34.3 us
    all_gather x1, waiting for transfers between devices, on_device(): rows = lax.all_gather(tokens, 'exp', axis=0, tiled=True)  31.8 us
    dot_general x4, matrix products, on_device(): lax.dot_general(parts[member], down[member], (((1,), (1,)), ((), ())), pr...  28.5 us
    all_gather x1, blocking collectives, on_device(): share = lax.all_gather(share, 'exp', axis=0, tiled=True)  14.9 us
    dot_general x4, matrix products, on_device(): jnp.dot(rows, gate_up[0, member], preferred_element_type=jnp.float32)  13.1 us
  transfers between devices with their start and end apart: 4, of which 4 were waited for; matrix products, arithmetic and copies ran while one was open for 6% of the time, Pallas kernels for 0%

profile of v1, /device:TPU:0, one launch (start us, length us, event | category | flops | bytes accessed | tf_op | source)
XLA Modules:
  0.0 257.1 jit_solution(3571631320095984755)
XLA Ops:
  6.5 0.0 all-gather.6.cloned.1.call-start
  6.5 0.7 all-gather.6.cloned.1.call-update
  7.3 0.0 all-gather.4.cloned.1.call-start
  7.3 0.0 copy-start.1
  7.3 0.0 copy-start.3
  7.3 0.0 copy-start.2
  7.3 2.7 %pad_maximum_fusion = bf16[2,4,256,384]{3,2,1,0:T(8,128)(2,1)} fusion(bf16[1,4,256,384]{3,2,1,0:T(8,128)(2,1)} %bitcast.146, bf16[1,4,256,384]{3,2,1,0:T(8,128)(2,1)} %bitcast.147), kind=kLoop, calls=%fused_computation.24 | loop fusion | flops 786432 | bytes 3145728 | tf_op jit(solution)/shard_map/stack | solution.py:19
  10.1 0.0 all-gather.4.cloned.1.call-update
  10.1 0.0 all-gather.8.cloned.1.call-start
  10.1 0.7 all-gather.8.cloned.1.call-update
  10.8 0.0 reduce-scatter.2.cloned.1.call-start
  10.9 0.0 copy-done.1
  10.9 0.0 copy-done.3
  10.9 0.1 select_reduce_fusion.1
  11.0 0.0 copy-done.2
  11.0 14.9 %all_gather.14 = f32[512,16]{0,1:T(8,128)S(1)} all-gather(f32[128,16]{0,1:T(8,128)S(1)} %select_reduce_fusion), channel_id=1, replica_groups=mesh['rep'=8,'exp'=4] {'exp'}, dimensions={0}, use_global_device_ids=true | all-gather | bytes 40960 | tf_op jit(solution)/shard_map/all_gather | solution.py:17
  25.9 31.8 %all-gather.6.cloned.1.call-done = bf16[512,2048]{1,0:T(8,128)(2,1)} async-done(((bf16[128,2048]{1,0:T(8,128)(2,1)}), bf16[512,2048]{1,0:T(8,128)(2,1)}) %all-gather.6.cloned.1.call-update) | async-done | bytes 2097168 | tf_op jit(solution)/shard_map/all_gather | solution.py:16
  57.7 0.0 copy-start
  57.7 72.8 %all-gather.4.cloned.1.call-done = bf16[2,4,2048,384]{3,2,1,0:T(8,128)(2,1)} async-done(((bf16[2,4,256,384]{3,2,1,0:T(8,128)(2,1)}), bf16[2,4,2048,384]{3,2,1,0:T(8,128)(2,1)}) %all-gather.4.cloned.1.call-update) | async-done | bytes 12582928 | tf_op jit(solution)/shard_map/all_gather | solution.py:19
  130.5 3.1 %fusion.17 = f32[512,384]{0,1:T(8,128)S(1)} fusion(bf16[512,2048]{1,0:T(8,128)(2,1)} %all-gather.6.cloned.1.call-done, bf16[2,4,2048,384]{3,2,1,0:T(8,128)(2,1)} %all-gather.4.cloned.1.call-done), kind=kOutput, calls=%fused_computation.31 | convolution fusion | flops 805306368 | bytes 4456448 | tf_op jit(solution)/shard_map/dot_general | solution.py:23
  133.6 0.0 copy-done
  133.6 3.3 %fusion.15 = f32[512,384]{0,1:T(8,128)} fusion(bf16[512,2048]{1,0:T(8,128)(2,1)S(1)} %copy-done, bf16[2,4,2048,384]{3,2,1,0:T(8,128)(2,1)} %all-gather.4.cloned.1.call-done), kind=kOutput, calls=%fused_computation.29 | convolution fusion | flops 805306368 | bytes 4456448 | tf_op jit(solution)/shard_map/dot_general | solution.py:23
  136.9 3.3 %fusion.13 = f32[512,384]{0,1:T(8,128)} fusion(bf16[512,2048]{1,0:T(8,128)(2,1)S(1)} %copy-done, bf16[2,4,2048,384]{3,2,1,0:T(8,128)(2,1)} %all-gather.4.cloned.1.call-done), kind=kOutput, calls=%fused_computation.27 | convolution fusion | flops 805306368 | bytes 4456448 | tf_op jit(solution)/shard_map/dot_general | solution.py:23
  140.2 3.4 %fusion.11 = f32[512,384]{0,1:T(8,128)} fusion(bf16[512,2048]{1,0:T(8,128)(2,1)S(1)} %copy-done, bf16[2,4,2048,384]{3,2,1,0:T(8,128)(2,1)} %all-gather.4.cloned.1.call-done), kind=kOutput, calls=%fused_computation.25 | convolution fusion | flops 805306368 | bytes 4456448 | tf_op jit(solution)/shard_map/dot_general | solution.py:23
  143.7 34.3 %all-gather.8.cloned.1.call-done = bf16[4,2048,384]{2,1,0:T(8,128)(2,1)} async-done(((bf16[4,256,384]{2,1,0:T(8,128)(2,1)}), bf16[4,2048,384]{2,1,0:T(8,128)(2,1)}) %all-gather.8.cloned.1.call-update) | async-done | bytes 6291472 | tf_op jit(solution)/shard_map/all_gather | solution.py:20
  178.0 6.4 %fusion.8 = f32[512,2048]{1,0:T(8,128)} fusion(bf16[4,2048,384]{2,1,0:T(8,128)(2,1)} %all-gather.8.cloned.1.call-done, bf16[512,2048]{1,0:T(8,128)(2,1)S(1)} %copy-done, bf16[2,4,2048,384]{3,2,1,0:T(8,128)(2,1)} %all-gather.4.cloned.1.call-done, f32[512,384]{0,1:T(8,128)} %fusion.11, f32[512]{0:T(512)S(1)} %bitcast.151), kind=kOutput, calls=%fused_computation.19 | convolution fusion | flops 1611988992 | bytes 10225664 | tf_op jit(solution)/shard_map/dot_general | solution.py:29
  184.4 6.4 %fusion.5 = f32[512,2048]{1,0:T(8,128)} fusion(bf16[4,2048,384]{2,1,0:T(8,128)(2,1)} %all-gather.8.cloned.1.call-done, bf16[512,2048]{1,0:T(8,128)(2,1)S(1)} %copy-done, bf16[2,4,2048,384]{3,2,1,0:T(8,128)(2,1)} %all-gather.4.cloned.1.call-done, f32[512,384]{0,1:T(8,128)} %fusion.13, f32[512]{0:T(512)S(1)} %bitcast.150), kind=kOutput, calls=%fused_computation.13 | convolution fusion | flops 1611988992 | bytes 10225664 | tf_op jit(solution)/shard_map/dot_general | solution.py:29
  190.9 6.5 %fusion.2 = f32[512,2048]{1,0:T(8,128)} fusion(bf16[4,2048,384]{2,1,0:T(8,128)(2,1)} %all-gather.8.cloned.1.call-done, bf16[512,2048]{1,0:T(8,128)(2,1)S(1)} %copy-done, bf16[2,4,2048,384]{3,2,1,0:T(8,128)(2,1)} %all-gather.4.cloned.1.call-done, f32[512,384]{0,1:T(8,128)} %fusion.15, f32[512]{0:T(512)S(1)} %bitcast.149), kind=kOutput, calls=%fused_computation.7 | convolution fusion | flops 1611988992 | bytes 10225664 | tf_op jit(solution)/shard_map/dot_general | solution.py:29
  197.3 9.2 %add_convert_fusion = bf16[512,2048]{1,0:T(8,128)(2,1)} fusion(f32[512,2048]{1,0:T(8,128)} %fusion.2, f32[512,2048]{1,0:T(8,128)} %fusion.8, f32[512,2048]{1,0:T(8,128)} %fusion.5, bf16[4,2048,384]{2,1,0:T(8,128)(2,1)} %all-gather.8.cloned.1.call-done, bf16[512,2048]{1,0:T(8,128)(2,1)S(1)} %copy-done, ...), kind=kOutput, calls=%fused_computation | convolution fusion | flops 1616183296 | bytes 20711424 | tf_op jit(solution)/shard_map/dot_general | solution.py:29
  206.5 0.0 reduce-scatter.2.cloned.1.call-update
  206.5 44.0 %reduce-scatter.2.cloned.1.call-done = bf16[128,2048]{1,0:T(8,128)(2,1)} async-done(((bf16[512,2048]{1,0:T(8,128)(2,1)}), bf16[128,2048]{1,0:T(8,128)(2,1)}) %reduce-scatter.2.cloned.1.call-update) | async-done | bytes 524304 | tf_op jit(solution)/shard_map/reduce_scatter | solution.py:32
  (2 shorter events, 0.0 us)
Async XLA Ops:
  6.5 51.2 %all-gather.6.cloned.1.call-start = ((), (), s32[]{:S(2)}) async-start(), calls=%async_computation.2 | async-start | bytes 2621440 | tf_op jit(solution)/shard_map/all_gather | solution.py:16
  7.3 123.3 %all-gather.4.cloned.1.call-start = ((), (), s32[]{:S(2)}) async-start(), calls=%async_computation.1 | async-start | bytes 14155776 | tf_op jit(solution)/shard_map/all_gather | solution.py:19
  7.3 3.6 %copy-start.1 = (s32[128,8]{0,1:T(8,128)S(1)}, s32[128,8]{0,1:T(8,128)}, u32[]{:S(2)}) copy-start(s32[128,8]{0,1:T(8,128)} %param.8) | copy-start | bytes 12292
  7.3 3.6 %copy-start.3 = (s32[16]{0:T(128)S(1)}, s32[16]{0:T(128)}, u32[]{:S(2)}) copy-start(s32[16]{0:T(128)} %param.10) | copy-start | bytes 196
  7.3 3.7 %copy-start.2 = (f32[128,8]{0,1:T(8,128)S(1)}, f32[128,8]{0,1:T(8,128)}, u32[]{:S(2)}) copy-start(f32[128,8]{0,1:T(8,128)} %param.9) | copy-start | bytes 12292
  10.1 167.9 %all-gather.8.cloned.1.call-start = ((), (), s32[]{:S(2)}) async-start(), calls=%async_computation.3 | async-start | bytes 7077888 | tf_op jit(solution)/shard_map/all_gather | solution.py:20
  10.8 239.7 %reduce-scatter.2.cloned.1.call-start = ((), (), s32[]{:S(2)}) async-start(), calls=%async_computation.4 | async-start | bytes 2621440 | tf_op jit(solution)/shard_map/reduce_scatter | solution.py:32
  57.7 75.9 %copy-start = (bf16[512,2048]{1,0:T(8,128)(2,1)S(1)}, bf16[512,2048]{1,0:T(8,128)(2,1)}, u32[]{:S(2)}) copy-start(bf16[512,2048]{1,0:T(8,128)(2,1)} %all-gather.6.cloned.1.call-done) | copy-start | bytes 6291460
Sparse Core Ops, SparseCore 0:
  8.9 48.7 all-gather.5
  59.6 70.8 all-gather.3
  132.4 45.5 all-gather.7
  206.6 43.8 reduce-scatter.1

commit v2 on v1

v2 whole, which is shorter than its diff:
```python
import functools

import jax
import jax.numpy as jnp
from jax import lax
from jax.experimental import pallas as pl
from jax.experimental.pallas import tpu as pltpu
from jax.sharding import PartitionSpec as P

LANES = 128
MESH = pl.DeviceIdType.MESH


def flip(index, bit):
    return index + bit - 2 * bit * ((index // bit) % 2)


def flip_all(index, combo):
    bit = 1
    while bit <= combo:
        if combo & bit:
            index = flip(index, bit)
        bit *= 2
    return index


def top_stage(route, combo):
    return max(stage for stage, bit in enumerate(route) if combo & bit)


def kernel(
    reps, groups, cuts,
    tokens, ids, shares, places, w_gate, w_up, w_down,
    mixed,
    rows_buf, share_buf, gate_up, down, hidden, sums, returned,
    barrier_free_local, token_send, token_recv, share_send, share_recv,
    chunk_send, chunk_recv, back_send, back_recv,
):
    rep, grp = lax.axis_index("rep"), lax.axis_index("exp")
    local, slab, width = w_gate.shape
    tok, model = tokens.shape
    feats = slab // cuts
    total_rows = groups * tok
    chip_bits = [1 << i for i in range(1, reps.bit_length() - 1)]
    routes = [chip_bits + [1], chip_bits[::-1] + [1]]
    stages = len(chip_bits) + 1
    half, piece = slab // 2, feats // 2
    chunks = local + cuts

    def peer(distance):
        return lax.rem(grp + distance, groups)

    barrier = pltpu.get_barrier_semaphore()
    for bit in routes[0]:
        pl.semaphore_signal(barrier, inc=1, device_id=(flip(rep, bit), grp), device_id_type=MESH)
    for distance in range(1, groups):
        pl.semaphore_signal(barrier, inc=1, device_id=(rep, peer(distance)), device_id_type=MESH)

    lane = lax.broadcasted_iota(jnp.int32, (tok, LANES), 1)
    dense = jnp.zeros((tok, LANES), jnp.float32)
    for k in range(ids.shape[1]):
        dense = dense + jnp.where(lane == ids[:, k : k + 1], shares[:, k : k + 1], 0.0)
    share_buf[grp] = dense

    own_copies = [
        pltpu.make_async_copy(tokens, rows_buf.at[grp], barrier_free_local.at[0]),
        pltpu.make_async_copy(w_gate, gate_up.at[:, 0, pl.ds(rep * slab, slab)], barrier_free_local.at[1]),
        pltpu.make_async_copy(w_up, gate_up.at[:, 1, pl.ds(rep * slab, slab)], barrier_free_local.at[2]),
    ]
    for q in range(cuts):
        own_copies.append(
            pltpu.make_async_copy(
                w_down.at[:, pl.ds(q * feats, feats)],
                down.at[:, q, pl.ds(rep * feats, feats)],
                barrier_free_local.at[3 + q],
            )
        )
    pl.semaphore_wait(barrier, len(routes[0]) + groups - 1)

    def token_copy(distance):
        to = (rep, peer(distance))
        return (
            pltpu.make_async_remote_copy(
                tokens, rows_buf.at[grp], token_send.at[distance - 1], token_recv.at[distance - 1],
                device_id=to, device_id_type=MESH,
            ),
            pltpu.make_async_remote_copy(
                share_buf.at[grp], share_buf.at[grp], share_send.at[distance - 1], share_recv.at[distance - 1],
                device_id=to, device_id_type=MESH,
            ),
        )

    def spot(chunk, route, block):
        if chunk < local:
            return gate_up.at[chunk, :, pl.ds(block * slab + route * half, half)]
        return down.at[:, chunk - local, pl.ds(block * feats + route * piece, piece)]

    def parts(chunk, route, block, own):
        if chunk < local:
            at = pl.ds(block * slab + route * half, half)
            if own:
                mine = pl.ds(route * half, half)
                sources = [w_gate.at[chunk, mine], w_up.at[chunk, mine]]
            else:
                sources = [gate_up.at[chunk, 0, at], gate_up.at[chunk, 1, at]]
            return [(sources[0], gate_up.at[chunk, 0, at]), (sources[1], gate_up.at[chunk, 1, at])]
        target = spot(chunk, route, block)
        if own:
            q = chunk - local
            return [(w_down.at[:, pl.ds(q * feats + route * piece, piece)], target)]
        return [(target, target)]

    def pass_on(chunk, route, combo, first_stage):
        block = flip_all(rep, combo)
        for stage in range(first_stage, stages):
            bit = routes[route][stage]
            slot = (combo | bit) - 1
            for source, target in parts(chunk, route, block, combo == 0):
                pltpu.make_async_remote_copy(
                    source, target, chunk_send.at[chunk, route, slot], chunk_recv.at[chunk, route, slot],
                    device_id=(flip(rep, bit), grp), device_id_type=MESH,
                ).start()

    def arrival(chunk, route, combo):
        place = spot(chunk, route, flip_all(rep, combo))
        return pltpu.make_async_remote_copy(
            place, place, chunk_send.at[chunk, route, combo - 1], chunk_recv.at[chunk, route, combo - 1],
            device_id=(flip(rep, 1), grp), device_id_type=MESH,
        )

    def send_own(chunk):
        for route in range(2):
            pass_on(chunk, route, 0, 0)

    def take(chunk, stage):
        for combo in range(1, reps):
            for route in range(2):
                if top_stage(routes[route], combo) == stage:
                    arrival(chunk, route, combo).wait_recv()
                    pass_on(chunk, route, combo, stage + 1)

    block_rows = min(2 * tok, total_rows)
    span = block_rows // tok

    def wait_tokens():
        for distance in range(1, groups):
            origin = lax.rem(grp + groups - distance, groups)
            pltpu.make_async_remote_copy(
                rows_buf.at[origin], rows_buf.at[origin],
                token_send.at[distance - 1], token_recv.at[distance - 1],
                device_id=(rep, peer(distance)), device_id_type=MESH,
            ).wait_recv()
            pltpu.make_async_remote_copy(
                share_buf.at[origin], share_buf.at[origin],
                share_send.at[distance - 1], share_recv.at[distance - 1],
                device_id=(rep, peer(distance)), device_id_type=MESH,
            ).wait_recv()

    def run_gate_up(member):
        slot = grp * local + member

        @pl.loop(0, total_rows // block_rows)
        def _(i):
            at = pl.ds(i * span, span)
            x = rows_buf[at].reshape(block_rows, model)
            gate_value = jnp.dot(x, gate_up[member, 0], preferred_element_type=jnp.float32)
            up_value = jnp.dot(x, gate_up[member, 1], preferred_element_type=jnp.float32)
            dense_rows = share_buf[at].reshape(block_rows, LANES)
            weight = jnp.sum(jnp.where(places[...] == slot, dense_rows, 0.0), axis=1, keepdims=True)
            value = gate_value * up_value * weight / (1.0 + jnp.exp(-gate_value))
            hidden[member, pl.ds(i * block_rows, block_rows)] = value.astype(jnp.bfloat16)

    columns = reps * feats
    cols = min(512, columns)

    def back_copy(q, part, distance):
        at = pl.ds(part * cols, cols)
        return pltpu.make_async_remote_copy(
            sums.at[q, peer(distance), :, at],
            returned.at[q, distance - 1, :, at],
            back_send.at[q, part, distance - 1],
            back_recv.at[q, part, distance - 1],
            device_id=(rep, peer(distance)), device_id_type=MESH,
        )

    def run_down(q):
        for part in range(columns // cols):

            @pl.loop(0, total_rows // block_rows)
            def _(i):
                total = jnp.zeros((block_rows, cols), jnp.float32)
                for member in range(local):
                    total = total + lax.dot_general(
                        hidden[member, pl.ds(i * block_rows, block_rows)],
                        down[member, q, part * cols : (part + 1) * cols],
                        (((1,), (1,)), ((), ())),
                        preferred_element_type=jnp.float32,
                    )
                sums[q, pl.ds(i * span, span), :, part * cols : (part + 1) * cols] = (
                    total.astype(jnp.bfloat16).reshape(span, tok, cols)
                )

            for distance in range(1, groups):
                back_copy(q, part, distance).start()

    for distance in range(1, groups):
        for copy in token_copy(distance):
            copy.start()
    send_own(0)
    for copy in own_copies:
        copy.start()
    if chunks > 1:
        send_own(1)
    take(0, 0)
    gate_up_done = 0
    for chunk in range(chunks):
        if chunk + 2 < chunks:
            send_own(chunk + 2)
        if chunk + 1 < chunks:
            take(chunk + 1, 0)
        for stage in range(1, stages):
            take(chunk, stage)
        if chunk == 0:
            for copy in own_copies:
                copy.wait()
        ready = chunk - 1 if chunk < local else local
        if ready > 0 and gate_up_done == 0:
            wait_tokens()
        while gate_up_done < ready:
            run_gate_up(gate_up_done)
            gate_up_done += 1
        if chunk >= local:
            run_down(chunk - local)

    for q in range(cuts):
        for part in range(columns // cols):
            for distance in range(1, groups):
                back_copy(q, part, distance).wait_recv()
            value = sums[q, grp, :, part * cols : (part + 1) * cols].astype(jnp.float32)
            for distance in range(1, groups):
                value = value + returned[q, distance - 1, :, part * cols : (part + 1) * cols].astype(jnp.float32)
            value = value.astype(jnp.bfloat16)
            for j in range(cols // feats):
                start = (part * cols // feats + j) * slab + q * feats
                mixed[:, start : start + feats] = value[:, j * feats : (j + 1) * feats]

    for distance in range(1, groups):
        for copy in token_copy(distance):
            copy.wait_send()
    for chunk in range(chunks):
        for route in range(2):
            for combo in range(1, reps):
                arrival(chunk, route, combo).wait_send()
    for q in range(cuts):
        for part in range(columns // cols):
            for distance in range(1, groups):
                back_copy(q, part, distance).wait_send()


def on_device(tokens, expert_ids, route_weights, placement_map, w_gate, w_up, down_rows):
    reps, groups = lax.axis_size("rep"), lax.axis_size("exp")
    local, slab, width = w_gate.shape
    tok, model = tokens.shape
    cuts = max(1, slab // LANES)
    feats = slab // cuts
    columns = reps * feats
    parts = columns // min(512, columns)
    chunks = local + cuts
    places = jnp.pad(placement_map, (0, LANES - placement_map.shape[0]), constant_values=-1).reshape(1, LANES)
    vmem, anywhere = pl.BlockSpec(memory_space=pltpu.VMEM), pl.BlockSpec(memory_space=pl.ANY)
    dma = pltpu.SemaphoreType.DMA
    return pl.pallas_call(
        functools.partial(kernel, reps, groups, cuts),
        out_shape=jax.ShapeDtypeStruct((tok, model), jnp.bfloat16),
        in_specs=[vmem, vmem, vmem, vmem, anywhere, anywhere, anywhere],
        out_specs=vmem,
        scratch_shapes=[
            pltpu.VMEM((groups, tok, model), jnp.bfloat16),
            pltpu.VMEM((groups, tok, LANES), jnp.float32),
            pltpu.VMEM((local, 2, reps * slab, width), jnp.bfloat16),
            pltpu.VMEM((local, cuts, columns, width), jnp.bfloat16),
            pltpu.VMEM((local, groups * tok, width), jnp.bfloat16),
            pltpu.VMEM((cuts, groups, tok, columns), jnp.bfloat16),
            pltpu.VMEM((cuts, groups - 1, tok, columns), jnp.bfloat16),
            dma((3 + cuts,)),
            dma((groups - 1,)),
            dma((groups - 1,)),
            dma((groups - 1,)),
            dma((groups - 1,)),
            dma((chunks, 2, reps - 1)),
            dma((chunks, 2, reps - 1)),
            dma((cuts, parts, groups - 1)),
            dma((cuts, parts, groups - 1)),
        ],
        compiler_params=pltpu.CompilerParams(
            collective_id=0, has_side_effects=True, vmem_limit_bytes=56 * 2**20
        ),
        cost_estimate=pl.CostEstimate(
            flops=6 * groups * tok * local * model * width,
            bytes_accessed=6 * local * slab * width + 4 * tok * model,
            transcendentals=groups * tok * local * width,
        ),
    )(tokens, expert_ids, route_weights, places, w_gate, w_up, down_rows)


def solution(mesh):
    return jax.shard_map(
        on_device,
        mesh=mesh,
        in_specs=(
            P(("rep", "exp"), None),
            P(("rep", "exp"), None),
            P(("rep", "exp"), None),
            P(),
            P("exp", "rep", None),
            P("exp", "rep", None),
            P("exp", "rep", None),
        ),
        out_specs=P(("rep", "exp"), None),
        check_vma=False,
    )
```

time: 257 us -> 141 us (0.55)
  waiting for transfers between devices: 184 us -> 0 us
  Pallas kernels: 0 us -> 134 us
  matrix products: 41.7 us -> 0 us
  blocking collectives: 14.9 us -> 0 us
  between operations: 13.2 us -> 0.01 us
  local copies, waits for them, and re-layouts: 0.03 us -> 5.28 us
  other arithmetic: 2.83 us -> 0 us
    all_gather x3 -> x0, waiting for transfers between devices: 139 us -> none  [the longest x1 72.8 us: on_device(): lax.all_gather(jnp.stack([w_gate, w_up]), 'rep', axis=2, tiled=True)]
    pallas_call x0 -> x1, Pallas kernels: none -> 134 us  [on_device(): pl.pallas_call(functools.partial(kernel, reps, groups, cuts), out_shape=j...]
    reduce_scatter x1 -> x0, waiting for transfers between devices: 44 us -> none  [on_device(): lax.psum_scatter(total.astype(jnp.bfloat16), 'exp', scatter_dimension=0,...]
    dot_general x8 -> x0, matrix products: 41.7 us -> none  [the longest x4 28.5 us: on_device(): lax.dot_general(parts[member], down[member], (((1,), (1,)), ((), ())), pr...]
    all_gather x1 -> x0, blocking collectives: 14.9 us -> none  [on_device(): share = lax.all_gather(share, 'exp', axis=0, tiled=True)]
    unnamed x8 -> x5, local copies, waits for them, and re-layouts: 0.02 us -> 4.05 us
    another operation x1 -> x0, other arithmetic: 2.73 us -> none  [on_device(): jnp.stack([w_gate, w_up])]
  transfers between devices with their start and end apart: 4 -> 0, of which waited for: 4 -> 0; matrix products, arithmetic and copies ran while one was open for 6% -> 0% of each run, Pallas kernels for 0% -> 0%
where the time goes in v2:
time: 141 us; the launch traced here: 139 us
  Pallas kernels  134 us (95%)
  local copies, waits for them, and re-layouts  5.28 us (4%)
    pallas_call x1, Pallas kernels, on_device(): pl.pallas_call(functools.partial(kernel, reps, groups, cuts), out_shape=j...  134 us
    unnamed x5, local copies, waits for them, and re-layouts  4.05 us

profile of v2, /device:TPU:0, one launch (start us, length us, event | category | flops | bytes accessed | tf_op | source)
XLA Modules:
  0.0 139.1 jit_solution(5031387508789365865)
XLA Ops:
  0.0 1.2 pad_bitcast_fusion.places
  1.2 0.0 copy-start
  1.2 1.4 %copy.8.ids = s32[128,8]{1,0:T(8,128)} copy(s32[128,8]{0,1:T(8,128)} %param.8) | data formatting | bytes 8192 | tf_op args[1]
  2.7 0.0 copy-done
  2.7 0.7 copy.9.shares
  3.4 133.8 %shard_map.73 = bf16[128,2048]{1,0:T(8,128)(2,1)} custom-call(bf16[128,2048]{1,0:T(8,128)(2,1)} %tokens.1, s32[128,8]{1,0:T(8,128)} %copy.8.ids, f32[128,8]{1,0:T(8,128)} %copy.9.shares, s32[1,128]{1,0:T(1,128)} %pad_bitcast_fusion.places, bf16[4,256,384]{2,1,0:T(8,128)(2,1)} %w_gate.1, bf16[4,256,384]{2,1,0:T(8,128)(2,1)} %w_up.1, bf16[4,256,384]{2,1,0:T(8,128)(2,1)} %w_down.1), custom_call_target="tpu_custom_call" | custom-call | flops 9663676416 | bytes 3407872 | tf_op jit(solution)/shard_map/pallas_call | solution.py:272
  137.2 1.9 %copy.11 = bf16[128,2048]{1,0:T(8,128)(2,1)} copy(bf16[128,2048]{1,0:T(8,128)(2,1)} %shard_map.73) | data formatting | bytes 1048576
Async XLA Ops:
  1.2 1.4 %copy-start = (f32[128,8]{0,1:T(8,128)S(1)}, f32[128,8]{0,1:T(8,128)}, u32[]{:S(2)}) copy-start(f32[128,8]{0,1:T(8,128)} %param.9) | copy-start | bytes 12292

commit v3 on v2

v3 whole, which is shorter than its diff:
```python
import functools

import jax
import jax.numpy as jnp
from jax import lax
from jax.experimental import pallas as pl
from jax.experimental.pallas import tpu as pltpu
from jax.sharding import PartitionSpec as P

LANES = 128
MESH = pl.DeviceIdType.MESH


def flip(index, bit):
    return index + bit - 2 * bit * ((index // bit) % 2)


def flip_all(index, combo):
    bit = 1
    while bit <= combo:
        if combo & bit:
            index = flip(index, bit)
        bit *= 2
    return index


def top_stage(route, combo):
    return max(stage for stage, bit in enumerate(route) if combo & bit)


def kernel(
    reps, groups, cuts,
    tokens, ids, shares, placement, w_gate, w_up, w_down,
    mixed,
    rows_buf, share_buf, gate_up, down, hidden, sums, returned,
    local_sem, token_send, token_recv, share_send, share_recv,
    chunk_send, chunk_recv, back_send, back_recv,
):
    rep, grp = lax.axis_index("rep"), lax.axis_index("exp")
    local, slab, width = w_gate.shape
    tok, model = tokens.shape
    feats = slab // cuts
    total_rows = groups * tok
    chip_bits = [1 << i for i in range(1, reps.bit_length() - 1)]
    routes = [chip_bits + [1], chip_bits[::-1] + [1]]
    stages = len(chip_bits) + 1
    half, piece = slab // 2, feats // 2
    chunks = local + cuts

    masks = [(2 << i) - 1 for i in range(groups.bit_length() - 1)]
    paths = {0: ()}
    for mask in masks:
        paths.update({at ^ mask: path + (mask,) for at, path in list(paths.items())})

    barrier = pltpu.get_barrier_semaphore()
    for bit in routes[0]:
        pl.semaphore_signal(barrier, inc=1, device_id=(flip(rep, bit), grp), device_id_type=MESH)
    for mask in masks:
        pl.semaphore_signal(barrier, inc=1, device_id=(rep, flip_all(grp, mask)), device_id_type=MESH)

    row = lax.broadcasted_iota(jnp.int32, (LANES, tok), 0)
    dense = jnp.zeros((LANES, tok), jnp.float32)
    for k in range(ids.shape[0]):
        dense = dense + jnp.where(row == ids[k : k + 1, :], shares[k : k + 1, :], 0.0)
    lane = lax.broadcasted_iota(jnp.int32, (1, LANES), 1)
    places = jnp.full((1, LANES), -1, jnp.int32)
    for expert in range(placement.shape[0]):
        places = jnp.where(lane == expert, placement[expert], places)
    share_buf[grp] = dense.T

    own_copies = [
        pltpu.make_async_copy(tokens, rows_buf.at[grp], local_sem.at[0]),
        pltpu.make_async_copy(w_gate, gate_up.at[:, 0, pl.ds(rep * slab, slab)], local_sem.at[1]),
        pltpu.make_async_copy(w_up, gate_up.at[:, 1, pl.ds(rep * slab, slab)], local_sem.at[2]),
    ]
    for q in range(cuts):
        own_copies.append(
            pltpu.make_async_copy(
                w_down.at[:, pl.ds(q * feats, feats)],
                down.at[:, q, pl.ds(rep * feats, feats)],
                local_sem.at[3 + q],
            )
        )
    pl.semaphore_wait(barrier, len(routes[0]) + len(masks))

    def token_copies(offset, mask):
        block, slot, to = flip_all(grp, offset), (offset ^ mask) - 1, (rep, flip_all(grp, mask))
        source = tokens if offset == 0 else rows_buf.at[block]
        return (
            pltpu.make_async_remote_copy(
                source, rows_buf.at[block], token_send.at[slot], token_recv.at[slot],
                device_id=to, device_id_type=MESH,
            ),
            pltpu.make_async_remote_copy(
                share_buf.at[block], share_buf.at[block], share_send.at[slot], share_recv.at[slot],
                device_id=to, device_id_type=MESH,
            ),
        )

    def token_arrivals(offset):
        block, slot, to = flip_all(grp, offset), offset - 1, (rep, flip_all(grp, 1))
        return (
            pltpu.make_async_remote_copy(
                rows_buf.at[block], rows_buf.at[block], token_send.at[slot], token_recv.at[slot],
                device_id=to, device_id_type=MESH,
            ),
            pltpu.make_async_remote_copy(
                share_buf.at[block], share_buf.at[block], share_send.at[slot], share_recv.at[slot],
                device_id=to, device_id_type=MESH,
            ),
        )

    def send_tokens(offset):
        least = min(paths[offset], default=groups)
        for mask in masks[::-1]:
            if mask < least:
                for copy in token_copies(offset, mask):
                    copy.start()

    def take_tokens(last):
        for offset in sorted(range(1, groups), key=lambda at: len(paths[at])):
            if (min(paths[offset]) == 1) == last:
                for copy in token_arrivals(offset):
                    copy.wait_recv()
                send_tokens(offset)

    def spot(chunk, route, block):
        if chunk < local:
            return gate_up.at[chunk, :, pl.ds(block * slab + route * half, half)]
        return down.at[:, chunk - local, pl.ds(block * feats + route * piece, piece)]

    def parts(chunk, route, block, own):
        if chunk < local:
            at = pl.ds(block * slab + route * half, half)
            if own:
                mine = pl.ds(route * half, half)
                sources = [w_gate.at[chunk, mine], w_up.at[chunk, mine]]
            else:
                sources = [gate_up.at[chunk, 0, at], gate_up.at[chunk, 1, at]]
            return [(sources[0], gate_up.at[chunk, 0, at]), (sources[1], gate_up.at[chunk, 1, at])]
        target = spot(chunk, route, block)
        if own:
            q = chunk - local
            return [(w_down.at[:, pl.ds(q * feats + route * piece, piece)], target)]
        return [(target, target)]

    def pass_on(chunk, route, combo, first_stage):
        block = flip_all(rep, combo)
        for stage in range(first_stage, stages):
            bit = routes[route][stage]
            slot = (combo | bit) - 1
            for source, target in parts(chunk, route, block, combo == 0):
                pltpu.make_async_remote_copy(
                    source, target, chunk_send.at[chunk, route, slot], chunk_recv.at[chunk, route, slot],
                    device_id=(flip(rep, bit), grp), device_id_type=MESH,
                ).start()

    def arrival(chunk, route, combo):
        place = spot(chunk, route, flip_all(rep, combo))
        return pltpu.make_async_remote_copy(
            place, place, chunk_send.at[chunk, route, combo - 1], chunk_recv.at[chunk, route, combo - 1],
            device_id=(flip(rep, 1), grp), device_id_type=MESH,
        )

    def send_own(chunk):
        for route in range(2):
            pass_on(chunk, route, 0, 0)

    def take(chunk, stage):
        for combo in range(1, reps):
            for route in range(2):
                if top_stage(routes[route], combo) == stage:
                    arrival(chunk, route, combo).wait_recv()
                    pass_on(chunk, route, combo, stage + 1)

    block_rows = min(2 * tok, total_rows)
    span = block_rows // tok

    def run_gate_up(member):
        @pl.loop(0, total_rows // block_rows)
        def _(i):
            at = pl.ds(i * span, span)
            x = rows_buf[at].reshape(block_rows, model)
            gate_value = jnp.dot(x, gate_up[member, 0], preferred_element_type=jnp.float32)
            up_value = jnp.dot(x, gate_up[member, 1], preferred_element_type=jnp.float32)
            value = gate_value * up_value / (1.0 + jnp.exp(-gate_value))
            hidden[member, pl.ds(i * block_rows, block_rows)] = value.astype(jnp.bfloat16)

    columns = reps * feats
    cols = min(512, columns)

    def back_copy(q, part, offset, mask):
        at = pl.ds(part * cols, cols)
        block = flip_all(grp, offset)
        slot = offset - 1
        return pltpu.make_async_remote_copy(
            sums.at[q, block, :, at],
            returned.at[q, slot, :, at],
            back_send.at[q, part, slot],
            back_recv.at[q, part, slot],
            device_id=(rep, flip_all(grp, mask)), device_id_type=MESH,
        )

    def with_first(mask):
        return sorted((at for at in paths if at and paths[at][0] == mask), key=lambda at: -len(paths[at]))

    def run_down(q, part):
        @pl.loop(0, total_rows // block_rows)
        def _(i):
            at = pl.ds(i * span, span)
            dense_rows = share_buf[at].reshape(block_rows, LANES)
            total = jnp.zeros((block_rows, cols), jnp.float32)
            for member in range(local):
                weight = jnp.sum(
                    jnp.where(places == grp * local + member, dense_rows, 0.0), axis=1, keepdims=True
                )
                total = total + weight * lax.dot_general(
                    hidden[member, pl.ds(i * block_rows, block_rows)],
                    down[member, q, part * cols : (part + 1) * cols],
                    (((1,), (1,)), ((), ())),
                    preferred_element_type=jnp.float32,
                )
            sums[q, at, :, part * cols : (part + 1) * cols] = total.astype(jnp.bfloat16).reshape(span, tok, cols)

        send_back(q, part, 0)

    def send_back(q, part, level):
        for offset in with_first(masks[level]):
            back_copy(q, part, offset, masks[level]).start()

    def merge_back(q, part, level):
        for offset in with_first(masks[level]):
            back_copy(q, part, offset, masks[level]).wait_recv()
        for offset in with_first(masks[level]):
            rest = offset ^ masks[level]
            if rest:
                back_copy(q, part, offset, masks[level]).wait_send()
                block = flip_all(grp, rest)
                at = slice(part * cols, (part + 1) * cols)
                sums[q, block, :, at] = (
                    sums[q, block, :, at].astype(jnp.float32) + returned[q, offset - 1, :, at].astype(jnp.float32)
                ).astype(jnp.bfloat16)
        if level + 1 < len(masks):
            send_back(q, part, level + 1)

    send_tokens(0)
    send_own(0)
    for copy in own_copies:
        copy.start()
    send_own(1)
    take(0, 0)
    pieces = [(q, part) for q in range(cuts) for part in range(columns // cols)]
    gate_up_done, merged, own_sent = 0, 0, 2
    for chunk in range(chunks):
        while own_sent < min(chunk + (3 if chunk + 2 < local else 4), chunks):
            send_own(own_sent)
            own_sent += 1
        if chunk + 1 < chunks:
            take(chunk + 1, 0)
        for stage in range(1, stages):
            take(chunk, stage)
        if chunk == 0:
            for copy in own_copies:
                copy.wait()
            take_tokens(False)
        if chunk == min(local - 1, 2):
            take_tokens(True)
        if chunk >= min(local - 1, 2):
            while gate_up_done < min(chunk + 1, local):
                run_gate_up(gate_up_done)
                gate_up_done += 1
        if chunk >= local:
            for part in range(columns // cols):
                run_down(chunk - local, part)
                now = pieces.index((chunk - local, part))
                if now - merged >= 1:
                    merge_back(*pieces[merged], 0)
                    merged += 1
    while merged < len(pieces):
        merge_back(*pieces[merged], 0)
        merged += 1
    for level in range(1, len(masks)):
        for piece_at in pieces:
            merge_back(*piece_at, level)

    for q, part in pieces:
        at = slice(part * cols, (part + 1) * cols)
        value = sums[q, grp, :, at].astype(jnp.float32)
        for mask in masks:
            value = value + returned[q, mask - 1, :, at].astype(jnp.float32)
        value = value.astype(jnp.bfloat16)
        for j in range(cols // feats):
            start = (part * cols // feats + j) * slab + q * feats
            mixed[:, start : start + feats] = value[:, j * feats : (j + 1) * feats]

    for offset in range(1, groups):
        for copy in token_arrivals(offset):
            copy.wait_send()
    for chunk in range(chunks):
        for route in range(2):
            for combo in range(1, reps):
                arrival(chunk, route, combo).wait_send()
    for q, part in pieces:
        for level, mask in enumerate(masks):
            for offset in with_first(mask):
                if offset == mask:
                    back_copy(q, part, offset, mask).wait_send()


def on_device(tokens, expert_ids, route_weights, placement_map, w_gate, w_up, down_rows):
    reps, groups = lax.axis_size("rep"), lax.axis_size("exp")
    local, slab, width = w_gate.shape
    tok, model = tokens.shape
    cuts = max(1, slab // 64)
    feats = slab // cuts
    columns = reps * feats
    parts = columns // min(512, columns)
    chunks = local + cuts
    vmem, anywhere = pl.BlockSpec(memory_space=pltpu.VMEM), pl.BlockSpec(memory_space=pl.ANY)
    dma = pltpu.SemaphoreType.DMA
    return pl.pallas_call(
        functools.partial(kernel, reps, groups, cuts),
        out_shape=jax.ShapeDtypeStruct((tok, model), jnp.bfloat16),
        in_specs=[vmem, vmem, vmem, pl.BlockSpec(memory_space=pltpu.SMEM), anywhere, anywhere, anywhere],
        out_specs=vmem,
        scratch_shapes=[
            pltpu.VMEM((groups, tok, model), jnp.bfloat16),
            pltpu.VMEM((groups, tok, LANES), jnp.float32),
            pltpu.VMEM((local, 2, reps * slab, width), jnp.bfloat16),
            pltpu.VMEM((local, cuts, columns, width), jnp.bfloat16),
            pltpu.VMEM((local, groups * tok, width), jnp.bfloat16),
            pltpu.VMEM((cuts, groups, tok, columns), jnp.bfloat16),
            pltpu.VMEM((cuts, groups - 1, tok, columns), jnp.bfloat16),
            dma((3 + cuts,)),
            dma((groups - 1,)),
            dma((groups - 1,)),
            dma((groups - 1,)),
            dma((groups - 1,)),
            dma((chunks, 2, reps - 1)),
            dma((chunks, 2, reps - 1)),
            dma((cuts, parts, groups - 1)),
            dma((cuts, parts, groups - 1)),
        ],
        compiler_params=pltpu.CompilerParams(
            collective_id=0, has_side_effects=True, vmem_limit_bytes=56 * 2**20
        ),
        cost_estimate=pl.CostEstimate(
            flops=6 * groups * tok * local * model * width,
            bytes_accessed=6 * local * slab * width + 4 * tok * model,
            transcendentals=groups * tok * local * width,
        ),
    )(tokens, expert_ids.T, route_weights.T, placement_map, w_gate, w_up, down_rows)


def solution(mesh):
    return jax.shard_map(
        on_device,
        mesh=mesh,
        in_specs=(
            P(("rep", "exp"), None),
            P(("rep", "exp"), None),
            P(("rep", "exp"), None),
            P(),
            P("exp", "rep", None),
            P("exp", "rep", None),
            P("exp", "rep", None),
        ),
        out_specs=P(("rep", "exp"), None),
        check_vma=False,
    )
```

time: 141 us -> 120 us (0.85)
  Pallas kernels: 134 us -> 117 us
  local copies, waits for them, and re-layouts: 5.28 us -> 1.88 us
    pallas_call x1, Pallas kernels: 134 us -> 117 us  [on_device(): pl.pallas_call(functools.partial(kernel, reps, groups, cuts), out_shape=j...]
    unnamed x5 -> x1, local copies, waits for them, and re-layouts: 4.05 us -> 1.88 us
where the time goes in v3:
time: 120 us; the launch traced here: 119 us
  Pallas kernels  117 us (98%)
  local copies, waits for them, and re-layouts  1.88 us (2%)
    pallas_call x1, Pallas kernels, on_device(): pl.pallas_call(functools.partial(kernel, reps, groups, cuts), out_shape=j...  117 us

profile of v3, /device:TPU:0, one launch (start us, length us, event | category | flops | bytes accessed | tf_op | source)
XLA Modules:
  0.0 119.2 jit_solution(4195954387594688146)
XLA Ops:
  0.0 117.3 %shard_map.73 = bf16[128,2048]{1,0:T(8,128)(2,1)} custom-call(bf16[128,2048]{1,0:T(8,128)(2,1)} %tokens.1, s32[8,128]{1,0:T(8,128)} %bitcast.2, f32[8,128]{1,0:T(8,128)} %bitcast.3, s32[16]{0:T(128)} %placement.1, bf16[4,256,384]{2,1,0:T(8,128)(2,1)} %w_gate.1, bf16[4,256,384]{2,1,0:T(8,128)(2,1)} %w_up.1, bf16[4,256,384]{2,1,0:T(8,128)(2,1)} %w_down.1), custom_call_target="tpu_custom_call" | custom-call | flops 9663676416 | bytes 3407872 | tf_op jit(solution)/shard_map/pallas_call | solution.py:321
  117.3 1.9 %copy.9 = bf16[128,2048]{1,0:T(8,128)(2,1)} copy(bf16[128,2048]{1,0:T(8,128)(2,1)} %shard_map.73) | data formatting | bytes 1048576

commit v4 on v3

--- a/solution.py
+++ b/solution.py
@@ -187,7 +187,7 @@
             hidden[member, pl.ds(i * block_rows, block_rows)] = value.astype(jnp.bfloat16)
 
     columns = reps * feats
-    cols = min(512, columns)
+    cols = min(256, columns)
 
     def back_copy(q, part, offset, mask):
         at = pl.ds(part * cols, cols)
@@ -257,15 +257,22 @@
             own_sent += 1
         if chunk + 1 < chunks:
             take(chunk + 1, 0)
+        first = min(local - 1, 2)
+        if chunk == first:
+            if chunk == 0:
+                take_tokens(False)
+            take_tokens(True)
         for stage in range(1, stages):
+            if chunk == first and gate_up_done < chunk:
+                run_gate_up(gate_up_done)
+                gate_up_done += 1
             take(chunk, stage)
         if chunk == 0:
             for copy in own_copies:
                 copy.wait()
-            take_tokens(False)
-        if chunk == min(local - 1, 2):
-            take_tokens(True)
-        if chunk >= min(local - 1, 2):
+            if first > 0:
+                take_tokens(False)
+        if chunk >= first:
             while gate_up_done < min(chunk + 1, local):
                 run_gate_up(gate_up_done)
                 gate_up_done += 1
@@ -273,17 +280,25 @@
             for part in range(columns // cols):
                 run_down(chunk - local, part)
                 now = pieces.index((chunk - local, part))
-                if now - merged >= 1:
+                if now - merged >= 2:
                     merge_back(*pieces[merged], 0)
                     merged += 1
+    for offset in range(1, groups):
+        for copy in token_arrivals(offset):
+            copy.wait_send()
+    for chunk in range(chunks):
+        for route in range(2):
+            for combo in range(1, reps):
+                arrival(chunk, route, combo).wait_send()
     while merged < len(pieces):
         merge_back(*pieces[merged], 0)
         merged += 1
-    for level in range(1, len(masks)):
+    for level in range(1, len(masks) - 1):
         for piece_at in pieces:
             merge_back(*piece_at, level)
 
     for q, part in pieces:
+        merge_back(q, part, len(masks) - 1)
         at = slice(part * cols, (part + 1) * cols)
         value = sums[q, grp, :, at].astype(jnp.float32)
         for mask in masks:
@@ -293,13 +308,6 @@
             start = (part * cols // feats + j) * slab + q * feats
             mixed[:, start : start + feats] = value[:, j * feats : (j + 1) * feats]
 
-    for offset in range(1, groups):
-        for copy in token_arrivals(offset):
-            copy.wait_send()
-    for chunk in range(chunks):
-        for route in range(2):
-            for combo in range(1, reps):
-                arrival(chunk, route, combo).wait_send()
     for q, part in pieces:
         for level, mask in enumerate(masks):
             for offset in with_first(mask):
@@ -314,7 +322,7 @@
     cuts = max(1, slab // 64)
     feats = slab // cuts
     columns = reps * feats
-    parts = columns // min(512, columns)
+    parts = columns // min(256, columns)
     chunks = local + cuts
     vmem, anywhere = pl.BlockSpec(memory_space=pltpu.VMEM), pl.BlockSpec(memory_space=pl.ANY)
     dma = pltpu.SemaphoreType.DMA

time: 120 us -> 118 us (0.983)
    pallas_call x1, Pallas kernels: 117 us -> 116 us  [on_device(): pl.pallas_call(functools.partial(kernel, reps, groups, cuts), out_shape=j...]
where the time goes in v4:
time: 118 us
  Pallas kernels  116 us (98%)
  local copies, waits for them, and re-layouts  1.88 us (2%)
    pallas_call x1, Pallas kernels, on_device(): pl.pallas_call(functools.partial(kernel, reps, groups, cuts), out_shape=j...  116 us

profile of v4, /device:TPU:0, one launch (start us, length us, event | category | flops | bytes accessed | tf_op | source)
XLA Modules:
  0.0 117.7 jit_solution(3031787205519645539)
XLA Ops:
  0.0 115.9 %shard_map.73 = bf16[128,2048]{1,0:T(8,128)(2,1)} custom-call(bf16[128,2048]{1,0:T(8,128)(2,1)} %tokens.1, s32[8,128]{1,0:T(8,128)} %bitcast.2, f32[8,128]{1,0:T(8,128)} %bitcast.3, s32[16]{0:T(128)} %placement.1, bf16[4,256,384]{2,1,0:T(8,128)(2,1)} %w_gate.1, bf16[4,256,384]{2,1,0:T(8,128)(2,1)} %w_up.1, bf16[4,256,384]{2,1,0:T(8,128)(2,1)} %w_down.1), custom_call_target="tpu_custom_call" | custom-call | flops 9663676416 | bytes 3407872 | tf_op jit(solution)/shard_map/pallas_call | solution.py:329
  115.9 1.9 %copy.9 = bf16[128,2048]{1,0:T(8,128)(2,1)} copy(bf16[128,2048]{1,0:T(8,128)(2,1)} %shard_map.73) | data formatting | bytes 1048576

commit v5 on v4

--- a/solution.py
+++ b/solution.py
@@ -110,19 +110,18 @@
             ),
         )
 
-    def send_tokens(offset):
+    def send_tokens(offset, over):
         least = min(paths[offset], default=groups)
-        for mask in masks[::-1]:
+        for mask in over:
             if mask < least:
                 for copy in token_copies(offset, mask):
                     copy.start()
 
-    def take_tokens(last):
-        for offset in sorted(range(1, groups), key=lambda at: len(paths[at])):
-            if (min(paths[offset]) == 1) == last:
-                for copy in token_arrivals(offset):
-                    copy.wait_recv()
-                send_tokens(offset)
+    def take_tokens(offsets):
+        for offset in sorted(offsets, key=lambda at: len(paths[at])):
+            for copy in token_arrivals(offset):
+                copy.wait_recv()
+            send_tokens(offset, masks[::-1])
 
     def spot(chunk, route, block):
         if chunk < local:
@@ -176,15 +175,18 @@
     block_rows = min(2 * tok, total_rows)
     span = block_rows // tok
 
-    def run_gate_up(member):
-        @pl.loop(0, total_rows // block_rows)
+    spans = groups // span
+
+    def run_gate_up(member, first, last):
+        @pl.loop(first, last)
         def _(i):
-            at = pl.ds(i * span, span)
+            turn = lax.rem(grp // span + i, spans)
+            at = pl.ds(turn * span, span)
             x = rows_buf[at].reshape(block_rows, model)
             gate_value = jnp.dot(x, gate_up[member, 0], preferred_element_type=jnp.float32)
             up_value = jnp.dot(x, gate_up[member, 1], preferred_element_type=jnp.float32)
             value = gate_value * up_value / (1.0 + jnp.exp(-gate_value))
-            hidden[member, pl.ds(i * block_rows, block_rows)] = value.astype(jnp.bfloat16)
+            hidden[member, pl.ds(turn * block_rows, block_rows)] = value.astype(jnp.bfloat16)
 
     columns = reps * feats
     cols = min(256, columns)
@@ -243,39 +245,47 @@
         if level + 1 < len(masks):
             send_back(q, part, level + 1)
 
-    send_tokens(0)
+    send_tokens(0, masks[:0:-1])
     send_own(0)
     for copy in own_copies:
         copy.start()
     send_own(1)
     take(0, 0)
+    send_tokens(0, masks[:1])
+    far = [offset for offset in range(1, groups) if min(paths[offset]) > 1]
     pieces = [(q, part) for q in range(cuts) for part in range(columns // cols)]
-    gate_up_done, merged, own_sent = 0, 0, 2
+    near_done, all_done, merged, own_sent = 0, 0, 0, 2
+    full = min(local - 1, 2)
     for chunk in range(chunks):
         while own_sent < min(chunk + (3 if chunk + 2 < local else 4), chunks):
             send_own(own_sent)
             own_sent += 1
         if chunk + 1 < chunks:
             take(chunk + 1, 0)
-        first = min(local - 1, 2)
-        if chunk == first:
-            if chunk == 0:
-                take_tokens(False)
-            take_tokens(True)
+        if chunk == full > 0:
+            take_tokens([offset for offset in range(2, groups) if offset not in far])
         for stage in range(1, stages):
-            if chunk == first and gate_up_done < chunk:
-                run_gate_up(gate_up_done)
-                gate_up_done += 1
+            if chunk == full and all_done < near_done:
+                run_gate_up(all_done, 1, spans)
+                all_done += 1
             take(chunk, stage)
         if chunk == 0:
             for copy in own_copies:
                 copy.wait()
-            if first > 0:
-                take_tokens(False)
-        if chunk >= first:
-            while gate_up_done < min(chunk + 1, local):
-                run_gate_up(gate_up_done)
-                gate_up_done += 1
+            take_tokens(far)
+            if full == 0:
+                take_tokens([offset for offset in range(1, groups) if offset not in far])
+        if chunk == 1 == full - 1:
+            take_tokens([1])
+            while near_done < 2:
+                run_gate_up(near_done, 0, 1)
+                near_done += 1
+        elif chunk == full == 1:
+            take_tokens([1])
+        if chunk >= full:
+            while all_done < min(chunk + 1, local):
+                run_gate_up(all_done, 1 if all_done < near_done else 0, spans)
+                all_done += 1
         if chunk >= local:
             for part in range(columns // cols):
                 run_down(chunk - local, part)

time: 118 us -> 118 us (level)
  no operation moved by 1% of the time
where the time goes in v5:
time: 118 us
  Pallas kernels  116 us (98%)
  local copies, waits for them, and re-layouts  1.88 us (2%)
    pallas_call x1, Pallas kernels, on_device(): pl.pallas_call(functools.partial(kernel, reps, groups, cuts), out_shape=j...  116 us

profile of v5, /device:TPU:0, one launch (start us, length us, event | category | flops | bytes accessed | tf_op | source)
XLA Modules:
  0.0 117.7 jit_solution(1762425541968157081)
XLA Ops:
  0.0 115.9 %shard_map.73 = bf16[128,2048]{1,0:T(8,128)(2,1)} custom-call(bf16[128,2048]{1,0:T(8,128)(2,1)} %tokens.1, s32[8,128]{1,0:T(8,128)} %bitcast.2, f32[8,128]{1,0:T(8,128)} %bitcast.3, s32[16]{0:T(128)} %placement.1, bf16[4,256,384]{2,1,0:T(8,128)(2,1)} %w_gate.1, bf16[4,256,384]{2,1,0:T(8,128)(2,1)} %w_up.1, bf16[4,256,384]{2,1,0:T(8,128)(2,1)} %w_down.1), custom_call_target="tpu_custom_call" | custom-call | flops 9663676416 | bytes 3407872 | tf_op jit(solution)/shard_map/pallas_call | solution.py:339
  115.9 1.9 %copy.9 = bf16[128,2048]{1,0:T(8,128)(2,1)} copy(bf16[128,2048]{1,0:T(8,128)(2,1)} %shard_map.73) | data formatting | bytes 1048576

commit v6 on v5

--- a/solution.py
+++ b/solution.py
@@ -32,7 +32,7 @@
     reps, groups, cuts,
     tokens, ids, shares, placement, w_gate, w_up, w_down,
     mixed,
-    rows_buf, share_buf, gate_up, down, hidden, sums, returned,
+    rows_buf, share_buf, weights, gate_up, down, hidden, sums, returned,
     local_sem, token_send, token_recv, share_send, share_recv,
     chunk_send, chunk_recv, back_send, back_recv,
 ):
@@ -206,28 +206,36 @@
     def with_first(mask):
         return sorted((at for at in paths if at and paths[at][0] == mask), key=lambda at: -len(paths[at]))
 
+    wide_rows = min(4 * tok, total_rows)
+    wide = wide_rows // tok
+
+    def spread_weights():
+        for member in range(local):
+
+            @pl.loop(0, groups)
+            def _(block):
+                kept = jnp.where(places == grp * local + member, share_buf[block], 0.0)
+                weights[member, block] = jnp.broadcast_to(jnp.sum(kept, axis=1, keepdims=True), (tok, LANES))
+
     def run_down(q, part):
-        @pl.loop(0, total_rows // block_rows)
+        @pl.loop(0, total_rows // wide_rows)
         def _(i):
-            at = pl.ds(i * span, span)
-            dense_rows = share_buf[at].reshape(block_rows, LANES)
-            total = jnp.zeros((block_rows, cols), jnp.float32)
+            at = pl.ds(i * wide, wide)
+            total = jnp.zeros((wide_rows, cols), jnp.float32)
             for member in range(local):
-                weight = jnp.sum(
-                    jnp.where(places == grp * local + member, dense_rows, 0.0), axis=1, keepdims=True
-                )
-                total = total + weight * lax.dot_general(
-                    hidden[member, pl.ds(i * block_rows, block_rows)],
+                weight = weights[member, at].reshape(wide_rows, LANES)
+                total = total + jnp.concatenate([weight] * (cols // LANES), axis=1) * lax.dot_general(
+                    hidden[member, pl.ds(i * wide_rows, wide_rows)],
                     down[member, q, part * cols : (part + 1) * cols],
                     (((1,), (1,)), ((), ())),
                     preferred_element_type=jnp.float32,
                 )
-            sums[q, at, :, part * cols : (part + 1) * cols] = total.astype(jnp.bfloat16).reshape(span, tok, cols)
-
-        send_back(q, part, 0)
-
-    def send_back(q, part, level):
+            sums[q, at, :, part * cols : (part + 1) * cols] = total.astype(jnp.bfloat16).reshape(wide, tok, cols)
+
+    def send_back(q, part, level, ends=(False, True)):
         for offset in with_first(masks[level]):
+            if (len(paths[offset]) == 1) not in ends:
+                continue
             back_copy(q, part, offset, masks[level]).start()
 
     def merge_back(q, part, level):
@@ -286,13 +294,25 @@
             while all_done < min(chunk + 1, local):
                 run_gate_up(all_done, 1 if all_done < near_done else 0, spans)
                 all_done += 1
+        if chunk == min(full, local - 1):
+            spread_weights()
         if chunk >= local:
             for part in range(columns // cols):
                 run_down(chunk - local, part)
+                send_back(chunk - local, part, 0, (False,) if chunk == chunks - 1 else (False, True))
                 now = pieces.index((chunk - local, part))
-                if now - merged >= 2:
+                if now - merged >= 2 and pieces[merged][0] < cuts - 1:
                     merge_back(*pieces[merged], 0)
                     merged += 1
+    for part in range(columns // cols):
+        send_back(cuts - 1, part, 0, (True,))
+    while merged < len(pieces):
+        merge_back(*pieces[merged], 0)
+        merged += 1
+    for level in range(1, len(masks) - 1):
+        for piece_at in pieces:
+            merge_back(*piece_at, level)
+
     for offset in range(1, groups):
         for copy in token_arrivals(offset):
             copy.wait_send()
@@ -300,12 +320,6 @@
         for route in range(2):
             for combo in range(1, reps):
                 arrival(chunk, route, combo).wait_send()
-    while merged < len(pieces):
-        merge_back(*pieces[merged], 0)
-        merged += 1
-    for level in range(1, len(masks) - 1):
-        for piece_at in pieces:
-            merge_back(*piece_at, level)
 
     for q, part in pieces:
         merge_back(q, part, len(masks) - 1)
@@ -344,6 +358,7 @@
         scratch_shapes=[
             pltpu.VMEM((groups, tok, model), jnp.bfloat16),
             pltpu.VMEM((groups, tok, LANES), jnp.float32),
+            pltpu.VMEM((local, groups, tok, LANES), jnp.float32),
             pltpu.VMEM((local, 2, reps * slab, width), jnp.bfloat16),
             pltpu.VMEM((local, cuts, columns, width), jnp.bfloat16),
             pltpu.VMEM((local, groups * tok, width), jnp.bfloat16),

time: 118 us -> 118 us (level)
  no operation moved by 1% of the time
where the time goes in v6:
time: 118 us
  Pallas kernels  116 us (98%)
  local copies, waits for them, and re-layouts  1.88 us (2%)
    pallas_call x1, Pallas kernels, on_device(): pl.pallas_call(functools.partial(kernel, reps, groups, cuts), out_shape=j...  116 us

profile of v6, /device:TPU:0, one launch (start us, length us, event | category | flops | bytes accessed | tf_op | source)
XLA Modules:
  0.0 117.9 jit_solution(18111847215930187001)
XLA Ops:
  0.0 116.0 %shard_map.73 = bf16[128,2048]{1,0:T(8,128)(2,1)} custom-call(bf16[128,2048]{1,0:T(8,128)(2,1)} %tokens.1, s32[8,128]{1,0:T(8,128)} %bitcast.2, f32[8,128]{1,0:T(8,128)} %bitcast.3, s32[16]{0:T(128)} %placement.1, bf16[4,256,384]{2,1,0:T(8,128)(2,1)} %w_gate.1, bf16[4,256,384]{2,1,0:T(8,128)(2,1)} %w_up.1, bf16[4,256,384]{2,1,0:T(8,128)(2,1)} %w_down.1), custom_call_target="tpu_custom_call" | custom-call | flops 9663676416 | bytes 3407872 | tf_op jit(solution)/shard_map/pallas_call | solution.py:353
  116.0 1.9 %copy.9 = bf16[128,2048]{1,0:T(8,128)(2,1)} copy(bf16[128,2048]{1,0:T(8,128)(2,1)} %shard_map.73) | data formatting | bytes 1048576

commit v7 on v6

--- a/solution.py
+++ b/solution.py
@@ -265,7 +265,7 @@
     near_done, all_done, merged, own_sent = 0, 0, 0, 2
     full = min(local - 1, 2)
     for chunk in range(chunks):
-        while own_sent < min(chunk + (3 if chunk + 2 < local else 4), chunks):
+        while own_sent < min(chunk + (3 if chunk < local else 4), chunks):
             send_own(own_sent)
             own_sent += 1
         if chunk + 1 < chunks:

time: 118 us -> 120 us (1.017)
  no operation moved by 1% of the time
where the time goes in v7:
time: 120 us; the launch traced here: 119 us
  Pallas kernels  117 us (98%)
  local copies, waits for them, and re-layouts  1.88 us (2%)
    pallas_call x1, Pallas kernels, on_device(): pl.pallas_call(functools.partial(kernel, reps, groups, cuts), out_shape=j...  117 us

profile of v7, /device:TPU:0, one launch (start us, length us, event | category | flops | bytes accessed | tf_op | source)
XLA Modules:
  0.0 118.8 jit_solution(2392940694338130862)
XLA Ops:
  0.0 116.9 %shard_map.73 = bf16[128,2048]{1,0:T(8,128)(2,1)} custom-call(bf16[128,2048]{1,0:T(8,128)(2,1)} %tokens.1, s32[8,128]{1,0:T(8,128)} %bitcast.2, f32[8,128]{1,0:T(8,128)} %bitcast.3, s32[16]{0:T(128)} %placement.1, bf16[4,256,384]{2,1,0:T(8,128)(2,1)} %w_gate.1, bf16[4,256,384]{2,1,0:T(8,128)(2,1)} %w_up.1, bf16[4,256,384]{2,1,0:T(8,128)(2,1)} %w_down.1), custom_call_target="tpu_custom_call" | custom-call | flops 9663676416 | bytes 3407872 | tf_op jit(solution)/shard_map/pallas_call | solution.py:353
  116.9 1.9 %copy.9 = bf16[128,2048]{1,0:T(8,128)(2,1)} copy(bf16[128,2048]{1,0:T(8,128)(2,1)} %shard_map.73) | data formatting | bytes 1048576
